TPU v7x, 32 devices: a whole 2x2x4 slice. The times are simulated.
32 devices in a mesh: pair: 32 (over z, y, x, core), sigma: 1.
Axes of the slice: x: 2, y: 2, z: 4, core: 2. Of those that a mesh axis runs over, the one named last changes fastest.
Arguments:
- pair_density_matrices: bfloat16 [65536, 1536], P('pair'), may hold values from -6 to 6
- energy_bins: int32 [65536, 2], P('pair'), may hold values from 0 to 63
- bin_weights: float32 [2, 64], replicated, may hold values from 0.05 to 1
- coulomb: float32 [1536], replicated, may hold values from 0.5 to 4
- state_matrices: bfloat16 [1536, 2048], P(None, 'sigma'), may hold values from -6 to 6
Outputs:
- screened_states: float32 [1536, 2, 2048], P('pair', None, 'sigma')
- sigma_diag: float32 [2, 2048], P(None, 'sigma')
All inputs are finite; a program needn't handle non-finite values.
Results may differ from a plain program's by a relative error of at most 0.00035.
Values sent between devices are 32-bit elements; how exact they have to be, the bound alone decides.
A program may use at most 128 MiB of HBM per device.

v0:
```python
import jax
import jax.numpy as jnp
from jax import lax
from jax.sharding import PartitionSpec as P


def pair_weights(energy_bins, bin_weights, pair_total):
    bin_levels = jnp.arange(bin_weights.shape[1], dtype=jnp.int32)
    matches = (energy_bins[:, :, None] == bin_levels[None, None, :]).astype(jnp.float32)
    picked = jnp.sum(matches * bin_weights[None, :, :], axis=2)
    return picked.T / jnp.float32(pair_total)


def local(pair_density_matrices, energy_bins, bin_weights, coulomb, state_matrices):
    pair_local, width = pair_density_matrices.shape
    pair_count = lax.axis_size("pair")
    self_energy_count = lax.axis_size("sigma")
    row_count = width // pair_count
    col_count = width // self_energy_count
    pair_position = lax.axis_index("pair")
    sigma_pos = lax.axis_index("sigma")
    weight = pair_weights(energy_bins, bin_weights, pair_local * pair_count)
    column_slab = lax.dynamic_slice_in_dim(
        pair_density_matrices, sigma_pos * col_count, col_count, 1
    )
    scaled_product = (weight[:, :, None] * column_slab[None, :, :].astype(jnp.float32)).astype(
        jnp.bfloat16
    )
    polar_block = lax.psum_scatter(
        -jnp.einsum(
            "zh,vzo->hvo", pair_density_matrices, scaled_product, preferred_element_type=jnp.float32
        ),
        "pair",
        scatter_dimension=0,
        tiled=True,
    )
    coulomb_root = jnp.sqrt(coulomb)
    root_rows = lax.dynamic_slice_in_dim(coulomb_root, pair_position * row_count, row_count, 0)
    coulomb_root_columns = lax.dynamic_slice_in_dim(
        coulomb_root, sigma_pos * col_count, col_count, 0
    )
    screened = root_rows[:, None, None] * polar_block * coulomb_root_columns[None, None, :]
    states_wide = state_matrices.astype(jnp.float32)
    applied = jnp.einsum(
        "rfc,cn->rfn",
        lax.all_gather(screened, "sigma", axis=2, tiled=True),
        states_wide,
        precision=lax.Precision.HIGHEST,
    )
    own_states = lax.dynamic_slice_in_dim(states_wide, pair_position * row_count, row_count, 0)
    partial_contribution = jnp.sum(own_states[:, None, :] * applied, axis=0) / jnp.float32(width)
    sigma_diag = lax.psum(partial_contribution, "pair")
    return (applied, sigma_diag)


def solution(mesh):
    return jax.shard_map(
        local,
        mesh=mesh,
        in_specs=(P("pair", None), P("pair", None), P(), P(), P(None, "sigma")),
        out_specs=(P("pair", None, "sigma"), P(None, "sigma")),
        check_vma=False,
    )
```

profile of v0, /device:TPU:0, one launch (start us, length us, event | category | flops | bytes accessed | tf_op | source)
XLA Modules:
  0.0 307.0 jit_solution(5319071559462647396)
XLA Ops:
  7.2 0.0 copy-start.2
  7.2 0.0 copy-start
  7.2 0.0 reduce-scatter.2.cloned.1.call-start
  7.2 9.2 %convert_element_type.11 = f32[2048,1536]{1,0:T(8,128)} convert(bf16[2048,1536]{1,0:T(8,128)(2,1)} %param.5) | non-fusion elementwise | flops 3145728 | bytes 18874368 | tf_op jit(solution)/shard_map/convert_element_type | solution.py:26
  16.4 0.0 copy-done.2
  16.4 0.0 copy-done
  16.4 0.3 select_reduce_fusion
  16.7 29.3 %negate_bitcast_fusion = f32[1536,2,1536]{2,0,1:T(8,128)} fusion(f32[2048,1536]{1,0:T(8,128)} %convert_element_type.11, f32[2,2048]{1,0:T(2,128)S(1)} %multiply_bitcast_fusion, bf16[2048,1536]{1,0:T(8,128)(2,1)} %param.5), kind=kOutput, calls=%fused_computation.1 | convolution fusion | flops 19344654336 | bytes 37765120 | tf_op jit(solution)/shard_map/zh,vzo->hvo/dot_general | solution.py:30
  46.0 0.0 copy-start.1
  46.0 0.0 reduce-scatter.2.cloned.1.call-update
  46.0 0.7 copy-done.1
  46.7 0.1 dynamic_slice.8
  46.7 1.0 dynamic-slice_convert_fusion
  47.7 206.2 %reduce-scatter.2.cloned.1.call-done = f32[48,2,1536]{2,0,1:T(8,128)} async-done(((f32[1536,2,1536]{2,0,1:T(8,128)}), f32[48,2,1536]{2,0,1:T(8,128)}) %reduce-scatter.2.cloned.1.call-update) | async-done | bytes 589840 | tf_op jit(solution)/shard_map/reduce_scatter | solution.py:29
  253.9 5.6 %multiply_reduce_fusion = (f32[2,2048]{1,0:T(2,128)S(1)}, f32[48,2,2048]{2,0,1:T(8,128)S(1)}) fusion(f32[48,2048]{1,0:T(8,128)S(1)} %dynamic-slice_convert_fusion, bf16[1536,2048]{1,0:T(8,128)(2,1)} %param.9, f32[48,2,1536]{2,0,1:T(8,128)} %reduce-scatter.2.cloned.1.call-done, f32[1536]{0:T(1024)S(1)} %sqrt.3, f32[48]{0:T(128)S(1)} %dynamic_slice.8), kind=kOutput, calls=%fused_computation.9 | convolution fusion | flops 3624562688 | bytes 8083648 | tf_op jit(solution)/shard_map/rfc,cn->rfn/dot_general | solution.py:44
  259.5 1.5 copy.10
  261.0 39.2 %psum.7 = f32[2,2048]{1,0:T(2,128)} all-reduce(f32[2,2048]{1,0:T(2,128)S(1)} %broadcast_multiply_fusion), channel_id=1, replica_groups=mesh['pair'=32,'sigma'=1] {'pair'}, use_global_device_ids=true, to_apply=%region_3.0 | all-reduce | flops 4096 | bytes 32768 | tf_op jit(solution)/shard_map/psum | solution.py:52
  (3 shorter events, 0.0 us)
Async XLA Ops:
  7.2 9.2 %copy-start.2 = (f32[2,64]{1,0:T(2,128)S(1)}, f32[2,64]{1,0:T(2,128)}, u32[]{:S(2)}) copy-start(f32[2,64]{1,0:T(2,128)} %param.7) | copy-start | bytes 1540
  7.2 9.2 %copy-start = (s32[2048,2]{0,1:T(2,128)S(1)}, s32[2048,2]{0,1:T(2,128)}, u32[]{:S(2)}) copy-start(s32[2048,2]{0,1:T(2,128)} %param.6) | copy-start | bytes 49156
  7.2 246.7 %reduce-scatter.2.cloned.1.call-start = ((), (), s32[]{:S(2)}) async-start(), calls=%async_computation.1 | async-start | bytes 19464192 | tf_op jit(solution)/shard_map/reduce_scatter | solution.py:29
  46.0 0.7 copy-start.1
Sparse Core Ops, SparseCore 0:
  46.1 207.7 reduce-scatter.1
where the time goes:
time: 307 us
  waiting for transfers between devices  206 us (67%)
  blocking collectives  39.2 us (13%)
  matrix products  34.9 us (11%)
  between operations  14.1 us (5%)
  other arithmetic  10.4 us (3%)
    reduce_scatter x1, waiting for transfers between devices, local(): lax.psum_scatter(-jnp.einsum('zh,vzo->hvo', pair_density_matrices, scaled...  206 us
    psum x1, blocking collectives, local(): sigma_diag = lax.psum(partial_contribution, 'pair')  39.2 us
    dot_general x1, matrix products, local(): jnp.einsum('zh,vzo->hvo', pair_density_matrices, scaled_product, preferre...  29.3 us
    convert_element_type x1, other arithmetic, local(): column_slab[None, :, :].astype(jnp.float32)  9.16 us
  transfers between devices with their start and end apart: 1, of which 1 were waited for; matrix products, arithmetic and copies ran while one was open for 0% of the time, Pallas kernels for 0%

commit v1 on v0

v1 whole, which is shorter than its diff:
```python
import functools

import jax
import jax.numpy as jnp
from jax import lax
from jax.experimental import pallas as pl
from jax.experimental.pallas import tpu as pltpu
from jax.sharding import PartitionSpec as P

MESH = pl.DeviceIdType.MESH
LANES = 128


def pair_weights(energy_bins, bin_weights, pair_total):
    bin_levels = jnp.arange(bin_weights.shape[1], dtype=jnp.int32)
    matches = (energy_bins[:, :, None] == bin_levels[None, None, :]).astype(jnp.float32)
    picked = jnp.sum(matches * bin_weights[None, :, :], axis=2)
    return picked / jnp.float32(pair_total)


def halving_orders(bits):
    first = list(range(bits))
    second = list(range(bits))
    if bits >= 4:
        first = [0, 1, 3, 2] + first[4:]
        second = [0, 2, 3, 1] + second[4:]
    return first, second


def place_in_order(block, order):
    place = 0
    for bit in order:
        place = place * 2 + ((block >> bit) & 1)
    return place


def flip(me, bit):
    own = lax.rem(me // (1 << bit), 2)
    return own, me + (1 << bit) * (1 - 2 * own)


def greet(me, bits):
    barrier = pltpu.get_barrier_semaphore()
    for bit in range(bits):
        pl.semaphore_signal(
            barrier, inc=1, device_id={"pair": flip(me, bit)[1]}, device_id_type=MESH
        )
    pl.semaphore_wait(barrier, bits)


def polar_kernel(bits, orders, lags, rows_ref, cols_ref, weight_ref, out_ref,
                 spread, scaled, prod, *rest):
    recv = rest[:bits]
    send_sem, recv_sem = rest[bits:]
    me = lax.axis_index("pair")
    freqs = len(orders)
    pairs, width = cols_ref.shape
    steps = width // LANES
    rows = out_ref.shape[1]
    half = (1 << bits) // 2
    piece = 256

    greet(me, bits)
    for f in range(freqs):
        spread[:, f * LANES:(f + 1) * LANES] = jnp.broadcast_to(
            weight_ref[:, f:f + 1], (pairs, LANES)
        )

    offsets = []
    for order in orders:
        at, found = 0, [0]
        for stage, bit in enumerate(order):
            at = at + flip(me, bit)[0] * ((1 << bits) >> (stage + 1))
            found.append(at)
        offsets.append(found)

    def copy_of(f, stage, t):
        bit = orders[f][stage]
        own, partner = flip(me, bit)
        size = (1 << bits) >> (stage + 1)
        start = offsets[f][stage] + (1 - own) * size
        return pltpu.make_async_remote_copy(
            src_ref=prod.at[f, t, pl.ds(start, size)],
            dst_ref=recv[stage].at[f, t],
            send_sem=send_sem.at[f, stage, t],
            recv_sem=recv_sem.at[f, stage, t],
            device_id={"pair": partner},
            device_id_type=MESH,
        )

    core = flip(me, 0)[0]

    def multiply(side, t):
        product = jnp.dot(rows_ref[side], scaled[...], preferred_element_type=jnp.float32)
        for k in range(half):
            for f in range(freqs):
                low = place_in_order(2 * k, orders[f])
                prod[f, t, low + side * half] = product[
                    k * rows:(k + 1) * rows, f * LANES:(f + 1) * LANES
                ]

    def body(step, carry):
        @pl.when(step < steps)
        def _():
            cols = pl.ds(pl.multiple_of(step * LANES, LANES), LANES)

            def scale(i, c):
                at = pl.ds(pl.multiple_of(i * piece, piece), piece)
                wide = cols_ref[at, cols].astype(jnp.float32)
                for f in range(freqs):
                    lane = slice(f * LANES, (f + 1) * LANES)
                    scaled[at, lane] = (spread[at, lane] * wide).astype(jnp.bfloat16)
                return c

            lax.fori_loop(0, pairs // piece, scale, 0)
            multiply(1 - core, step)
            for f in range(freqs):
                copy_of(f, 0, step).start()
            multiply(core, step)

        for stage in range(1, bits + 1):
            t = step - lags[stage]

            @pl.when(jnp.logical_and(t >= 0, t < steps))
            def _(stage=stage, t=t):
                size = (1 << bits) >> stage
                for f in range(freqs):
                    copy_of(f, stage - 1, t).wait_recv()
                    kept = pl.ds(offsets[f][stage], size)
                    if stage < bits:
                        prod[f, t, kept] += recv[stage - 1][f, t]
                        copy_of(f, stage, t).start()
                    else:
                        cols = pl.ds(pl.multiple_of(t * LANES, LANES), LANES)
                        out_ref[f, :, cols] = (
                            prod[f, t, offsets[f][stage]] + recv[stage - 1][f, t, 0]
                        )

        return carry

    lax.fori_loop(0, steps + lags[bits], body, 0)

    def finish(t, carry):
        for stage in range(bits):
            for f in range(freqs):
                copy_of(f, stage, t).wait_send()
        return carry

    lax.fori_loop(0, steps, finish, 0)


def polar_rows(pair_rows, columns, weight, pair_count):
    pairs, width = columns.shape
    total_rows = pair_rows.shape[1]
    freqs = weight.shape[1]
    bits = pair_count.bit_length() - 1
    rows = total_rows // pair_count
    steps = width // LANES
    orders = halving_orders(bits)
    lags = [0, 1] + [2 * k + 1 for k in range(1, bits)]
    by_core = pair_rows.reshape(pairs, pair_count // 2, 2, rows).transpose(2, 1, 3, 0)
    by_core = by_core.reshape(2, total_rows // 2, pairs)
    return pl.pallas_call(
        functools.partial(polar_kernel, bits, orders, lags),
        out_shape=jax.ShapeDtypeStruct((freqs, rows, width), jnp.float32),
        in_specs=[pl.BlockSpec(memory_space=pltpu.VMEM)] * 3,
        out_specs=pl.BlockSpec(memory_space=pltpu.VMEM),
        scratch_shapes=[
            pltpu.VMEM((pairs, freqs * LANES), jnp.float32),
            pltpu.VMEM((pairs, freqs * LANES), jnp.bfloat16),
            pltpu.VMEM((freqs, steps, pair_count, rows, LANES), jnp.float32),
        ]
        + [
            pltpu.VMEM((freqs, steps, pair_count >> (s + 1), rows, LANES), jnp.float32)
            for s in range(bits)
        ]
        + [
            pltpu.SemaphoreType.DMA((freqs, bits, steps)),
            pltpu.SemaphoreType.DMA((freqs, bits, steps)),
        ],
        compiler_params=pltpu.CompilerParams(
            collective_id=0, has_side_effects=True, vmem_limit_bytes=60 * 1024 * 1024
        ),
        cost_estimate=pl.CostEstimate(
            flops=2 * pairs * total_rows * width * freqs,
            bytes_accessed=4 * pairs * total_rows,
            transcendentals=0,
        ),
    )(by_core, columns, weight)


def total_kernel(bits, part_ref, out_ref, held, got, send_sem, recv_sem):
    me = lax.axis_index("pair")
    greet(me, bits)
    held[0] = part_ref[...]
    for bit in range(bits):
        copy = pltpu.make_async_remote_copy(
            src_ref=held.at[bit],
            dst_ref=got.at[bit],
            send_sem=send_sem.at[bit],
            recv_sem=recv_sem.at[bit],
            device_id={"pair": flip(me, bit)[1]},
            device_id_type=MESH,
        )
        copy.start()
        copy.wait()
        held[bit + 1] = held[bit] + got[bit]
    out_ref[...] = held[bits]


def pair_total(part, pair_count):
    bits = pair_count.bit_length() - 1
    return pl.pallas_call(
        functools.partial(total_kernel, bits),
        out_shape=jax.ShapeDtypeStruct(part.shape, jnp.float32),
        in_specs=[pl.BlockSpec(memory_space=pltpu.VMEM)],
        out_specs=pl.BlockSpec(memory_space=pltpu.VMEM),
        scratch_shapes=[
            pltpu.VMEM((bits + 1,) + part.shape, jnp.float32),
            pltpu.VMEM((bits,) + part.shape, jnp.float32),
            pltpu.SemaphoreType.DMA((bits,)),
            pltpu.SemaphoreType.DMA((bits,)),
        ],
        compiler_params=pltpu.CompilerParams(collective_id=1, has_side_effects=True),
    )(part)


def local(pair_density_matrices, energy_bins, bin_weights, coulomb, state_matrices):
    pair_local, width = pair_density_matrices.shape
    pair_count = lax.axis_size("pair")
    self_energy_count = lax.axis_size("sigma")
    row_count = width // pair_count
    col_count = width // self_energy_count
    pair_position = lax.axis_index("pair")
    sigma_pos = lax.axis_index("sigma")
    weight = pair_weights(energy_bins, bin_weights, pair_local * pair_count)
    column_slab = lax.dynamic_slice_in_dim(
        pair_density_matrices, sigma_pos * col_count, col_count, 1
    )
    polar_block = -polar_rows(pair_density_matrices, column_slab, weight, pair_count)
    coulomb_root = jnp.sqrt(coulomb)
    root_rows = lax.dynamic_slice_in_dim(coulomb_root, pair_position * row_count, row_count, 0)
    coulomb_root_columns = lax.dynamic_slice_in_dim(
        coulomb_root, sigma_pos * col_count, col_count, 0
    )
    screened = root_rows[None, :, None] * polar_block * coulomb_root_columns[None, None, :]
    states_wide = state_matrices.astype(jnp.float32)
    applied = jnp.einsum(
        "frc,cn->rfn",
        lax.all_gather(screened, "sigma", axis=2, tiled=True),
        states_wide,
        precision=lax.Precision.HIGHEST,
    )
    own_states = lax.dynamic_slice_in_dim(states_wide, pair_position * row_count, row_count, 0)
    partial_contribution = jnp.sum(own_states[:, None, :] * applied, axis=0) / jnp.float32(width)
    sigma_diag = pair_total(partial_contribution, pair_count)
    return (applied, sigma_diag)


def solution(mesh):
    return jax.shard_map(
        local,
        mesh=mesh,
        in_specs=(P("pair", None), P("pair", None), P(), P(), P(None, "sigma")),
        out_specs=(P("pair", None, "sigma"), P(None, "sigma")),
        check_vma=False,
    )
```

time: 307 us -> 140 us (0.46)
  waiting for transfers between devices: 206 us -> 0 us
  Pallas kernels: 0 us -> 112 us
  blocking collectives: 39.2 us -> 0 us
  matrix products: 34.9 us -> 5.55 us
  local copies, waits for them, and re-layouts: 2.24 us -> 18.5 us
  between operations: 14.1 us -> 0.69 us
  other arithmetic: 10.4 us -> 2.91 us
    reduce_scatter x1 -> x0, waiting for transfers between devices: 206 us -> none  [local(): lax.psum_scatter(-jnp.einsum('zh,vzo->hvo', pair_density_matrices, scaled...]
    pallas_call x0 -> x2, Pallas kernels: none -> 112 us  [the longest x1 97.5 us: polar_rows(): pl.pallas_call(functools.partial(polar_kernel, bits, orders, lags), out_s...]
    psum x1 -> x0, blocking collectives: 39.2 us -> none  [local(): sigma_diag = lax.psum(partial_contribution, 'pair')]
    dot_general x2 -> x1, matrix products: 34.9 us -> 5.55 us  [local(): jnp.einsum('frc,cn->rfn', lax.all_gather(screened, 'sigma', axis=2, tiled...]
    unnamed x7 -> x9, local copies, waits for them, and re-layouts: 2.16 us -> 11.5 us
    convert_element_type x1 -> x0, other arithmetic: 9.16 us -> none  [local(): column_slab[None, :, :].astype(jnp.float32)]
    transpose x0 -> x1, local copies, waits for them, and re-layouts: none -> 6.6 us  [polar_rows(): pair_rows.reshape(pairs, pair_count // 2, 2, rows).transpose(2, 1, 3, 0)]
  transfers between devices with their start and end apart: 1 -> 0, of which waited for: 1 -> 0; matrix products, arithmetic and copies ran while one was open for 0% -> 0% of each run, Pallas kernels for 0% -> 0%
where the time goes in v1:
time: 140 us
  Pallas kernels  112 us (80%)
  local copies, waits for them, and re-layouts  18.5 us (13%)
  matrix products  5.55 us (4%)
  other arithmetic  2.91 us (2%)
    pallas_call x1, Pallas kernels, polar_rows(): pl.pallas_call(functools.partial(polar_kernel, bits, orders, lags), out_s...  97.5 us
    pallas_call x1, Pallas kernels, pair_total(): pl.pallas_call(functools.partial(total_kernel, bits), out_shape=jax.Shape...  14.8 us
    unnamed x9, local copies, waits for them, and re-layouts  11.5 us
    transpose x1, local copies, waits for them, and re-layouts, polar_rows(): pair_rows.reshape(pairs, pair_count // 2, 2, rows).transpose(2, 1, 3, 0)  6.6 us
    dot_general x1, matrix products, local(): jnp.einsum('frc,cn->rfn', lax.all_gather(screened, 'sigma', axis=2, tiled...  5.55 us

profile of v1, /device:TPU:0, one launch (start us, length us, event | category | flops | bytes accessed | tf_op | source)
XLA Modules:
  0.0 140.0 jit_solution(9234733655597988333)
XLA Ops:
  0.6 1.0 dynamic-slice_convert_fusion
  1.6 8.7 %copy.18 = bf16[2048,1536]{0,1:T(8,128)(2,1)} copy(bf16[2048,1536]{1,0:T(8,128)(2,1)} %cols_ref) | data formatting | bytes 12582912 | tf_op args[0]
  10.3 0.0 copy-start
  10.3 0.0 copy-start.2
  10.3 6.6 %copy.19 = bf16[2,16,48,2048]{3,2,1,0:T(8,128)(2,1)} copy(bf16[2,16,48,2048]{3,2,0,1:T(8,128)(2,1)} %bitcast.13) | data formatting | bytes 12582912 | tf_op jit(solution)/shard_map/transpose | solution.py:161
  16.9 0.0 copy-done
  16.9 0.0 copy-done.2
  16.9 0.3 select_reduce_fusion
  17.1 0.4 copy.20
  17.5 1.1 broadcast_multiply_fusion.weight_ref
  18.6 0.0 copy-start.1
  18.6 97.5 %shard_map.68 = f32[2,48,1536]{2,1,0:T(8,128)} custom-call(bf16[2,768,2048]{2,1,0:T(8,128)(2,1)} %bitcast.14, bf16[2048,1536]{1,0:T(8,128)(2,1)} %cols_ref, f32[2048,2]{1,0:T(8,128)} %broadcast_multiply_fusion.weight_ref), custom_call_target="tpu_custom_call" | custom-call | flops 19327352832 | bytes 12582912 | tf_op jit(solution)/shard_map/pallas_call | solution.py:163
  116.1 0.0 copy-done.1
  116.1 0.1 dynamic_slice.8
  116.2 5.6 %multiply_reduce_fusion = (f32[2,2048]{1,0:T(2,128)S(1)}, f32[48,2,2048]{2,0,1:T(8,128)S(1)}) fusion(f32[48,2048]{1,0:T(8,128)S(1)} %dynamic-slice_convert_fusion, bf16[1536,2048]{1,0:T(8,128)(2,1)} %param.9, f32[2,48,1536]{2,1,0:T(8,128)} %shard_map.68, f32[1536]{0:T(1024)S(1)} %sqrt.3, f32[48]{0:T(128)S(1)} %dynamic_slice.8), kind=kOutput, calls=%fused_computation.5 | convolution fusion | flops 3624710144 | bytes 8083648 | tf_op jit(solution)/shard_map/frc,cn->rfn/dot_general | solution.py:248
  121.8 1.5 %copy.22 = f32[48,2,2048]{2,1,0:T(2,128)} copy(f32[48,2,2048]{2,0,1:T(8,128)S(1)} %get-tuple-element.11) | data formatting | bytes 1572864
  123.2 0.6 broadcast_multiply_fusion.1.part_ref
  123.9 14.8 %shard_map.69 = f32[2,2048]{1,0:T(2,128)} custom-call(f32[2,2048]{1,0:T(2,128)} %broadcast_multiply_fusion.1.part_ref), custom_call_target="tpu_custom_call" | custom-call | tf_op jit(solution)/shard_map/pallas_call | solution.py:213
  138.7 1.3 copy.24
  (1 shorter events, 0.0 us)
Async XLA Ops:
  10.3 6.6 %copy-start = (s32[2048,2]{0,1:T(2,128)S(1)}, s32[2048,2]{0,1:T(2,128)}, u32[]{:S(2)}) copy-start(s32[2048,2]{0,1:T(2,128)} %param.6) | copy-start | bytes 49156
  10.3 6.6 %copy-start.2 = (f32[2,64]{1,0:T(2,128)S(1)}, f32[2,64]{1,0:T(2,128)}, u32[]{:S(2)}) copy-start(f32[2,64]{1,0:T(2,128)} %param.7) | copy-start | bytes 1540
  18.6 97.5 %copy-start.1 = (f32[1536]{0:T(1024)S(1)}, f32[1536]{0:T(1024)}, u32[]{:S(2)}) copy-start(f32[1536]{0:T(1024)} %param.8) | copy-start | bytes 18436

commit v2 on v1

--- a/solution.py
+++ b/solution.py
@@ -48,8 +48,12 @@
     pl.semaphore_wait(barrier, bits)
 
 
-def polar_kernel(bits, orders, lags, rows_ref, cols_ref, weight_ref, out_ref,
-                 spread, scaled, prod, *rest):
+def polar_kernel(bits, orders, lags, slab, full_ref, *refs):
+    if slab is None:
+        cols_ref = full_ref
+    else:
+        cols_ref, *refs = refs
+    weight_ref, out_ref, spread, scaled, turned, prod, *rest = refs
     recv = rest[:bits]
     send_sem, recv_sem = rest[bits:]
     me = lax.axis_index("pair")
@@ -58,9 +62,16 @@
     steps = width // LANES
     rows = out_ref.shape[1]
     half = (1 << bits) // 2
+    half_rows = half * rows
     piece = 256
 
     greet(me, bits)
+    def turn(i, c):
+        lane = pl.ds(pl.multiple_of(i * LANES, LANES), LANES)
+        turned[lane, :] = full_ref[:, lane].T
+        return c
+
+    lax.fori_loop(0, full_ref.shape[1] // LANES, turn, 0)
     for f in range(freqs):
         spread[:, f * LANES:(f + 1) * LANES] = jnp.broadcast_to(
             weight_ref[:, f:f + 1], (pairs, LANES)
@@ -88,14 +99,15 @@
             device_id_type=MESH,
         )
 
-    core = flip(me, 0)[0]
-
     def multiply(side, t):
-        product = jnp.dot(rows_ref[side], scaled[...], preferred_element_type=jnp.float32)
+        product = jnp.dot(
+            turned[side * half_rows:(side + 1) * half_rows, :],
+            scaled[...],
+            preferred_element_type=jnp.float32,
+        )
         for k in range(half):
             for f in range(freqs):
-                low = place_in_order(2 * k, orders[f])
-                prod[f, t, low + side * half] = product[
+                prod[f, t, place_in_order(side * half + k, orders[f])] = product[
                     k * rows:(k + 1) * rows, f * LANES:(f + 1) * LANES
                 ]
 
@@ -113,10 +125,10 @@
                 return c
 
             lax.fori_loop(0, pairs // piece, scale, 0)
-            multiply(1 - core, step)
+            multiply(0, step)
+            multiply(1, step)
             for f in range(freqs):
                 copy_of(f, 0, step).start()
-            multiply(core, step)
 
         for stage in range(1, bits + 1):
             t = step - lags[stage]
@@ -149,25 +161,25 @@
     lax.fori_loop(0, steps, finish, 0)
 
 
-def polar_rows(pair_rows, columns, weight, pair_count):
-    pairs, width = columns.shape
-    total_rows = pair_rows.shape[1]
+def polar_rows(densities, slab, weight, pair_count):
+    pairs, total_rows = densities.shape
+    operands = [densities, weight] if slab is None else [densities, slab, weight]
+    width = total_rows if slab is None else slab.shape[1]
     freqs = weight.shape[1]
     bits = pair_count.bit_length() - 1
     rows = total_rows // pair_count
     steps = width // LANES
     orders = halving_orders(bits)
-    lags = [0, 1] + [2 * k + 1 for k in range(1, bits)]
-    by_core = pair_rows.reshape(pairs, pair_count // 2, 2, rows).transpose(2, 1, 3, 0)
-    by_core = by_core.reshape(2, total_rows // 2, pairs)
+    lags = [0, 1] + [k + 2 for k in range(1, bits)]
     return pl.pallas_call(
-        functools.partial(polar_kernel, bits, orders, lags),
+        functools.partial(polar_kernel, bits, orders, lags, None if slab is None else 0),
         out_shape=jax.ShapeDtypeStruct((freqs, rows, width), jnp.float32),
-        in_specs=[pl.BlockSpec(memory_space=pltpu.VMEM)] * 3,
+        in_specs=[pl.BlockSpec(memory_space=pltpu.VMEM)] * len(operands),
         out_specs=pl.BlockSpec(memory_space=pltpu.VMEM),
         scratch_shapes=[
             pltpu.VMEM((pairs, freqs * LANES), jnp.float32),
             pltpu.VMEM((pairs, freqs * LANES), jnp.bfloat16),
+            pltpu.VMEM((total_rows, pairs), jnp.bfloat16),
             pltpu.VMEM((freqs, steps, pair_count, rows, LANES), jnp.float32),
         ]
         + [
@@ -186,40 +198,78 @@
             bytes_accessed=4 * pairs * total_rows,
             transcendentals=0,
         ),
-    )(by_core, columns, weight)
-
-
-def total_kernel(bits, part_ref, out_ref, held, got, send_sem, recv_sem):
+    )(*operands)
+
+
+def total_kernel(near, far, part_ref, out_ref, held, got, got_far, send_sem, recv_sem):
     me = lax.axis_index("pair")
-    greet(me, bits)
-    held[0] = part_ref[...]
-    for bit in range(bits):
-        copy = pltpu.make_async_remote_copy(
-            src_ref=held.at[bit],
-            dst_ref=got.at[bit],
-            send_sem=send_sem.at[bit],
-            recv_sem=recv_sem.at[bit],
-            device_id={"pair": flip(me, bit)[1]},
-            device_id_type=MESH,
-        )
-        copy.start()
-        copy.wait()
-        held[bit + 1] = held[bit] + got[bit]
-    out_ref[...] = held[bits]
+    low, high = lax.rem(me, near), me // near
+    groups = []
+    for k in range(1, near):
+        slot = lax.rem(low + k, near)
+        groups.append((slot, high * near + slot))
+    groups_far = []
+    for k in range(1, far):
+        slot = lax.rem(high + k, far)
+        groups_far.append((slot, slot * near + low))
+
+    barrier = pltpu.get_barrier_semaphore()
+    for _, peer in groups + groups_far:
+        pl.semaphore_signal(barrier, inc=1, device_id={"pair": peer}, device_id_type=MESH)
+    pl.semaphore_wait(barrier, near + far - 2)
+
+    def exchange(source, slots, own, peers, base):
+        copies = []
+        for k, (slot, peer) in enumerate(peers):
+            copies.append(
+                pltpu.make_async_remote_copy(
+                    src_ref=source,
+                    dst_ref=slots.at[own],
+                    send_sem=send_sem.at[base + k],
+                    recv_sem=recv_sem.at[base + own],
+                    device_id={"pair": peer},
+                    device_id_type=MESH,
+                )
+            )
+            copies[-1].start()
+        slots[own] = source[...]
+        for slot, _ in peers:
+            pltpu.make_async_remote_copy(
+                src_ref=source,
+                dst_ref=slots.at[slot],
+                send_sem=send_sem.at[base],
+                recv_sem=recv_sem.at[base + slot],
+                device_id={"pair": peers[0][1]},
+                device_id_type=MESH,
+            ).wait_recv()
+        total = slots[0]
+        for k in range(1, len(peers) + 1):
+            total = total + slots[k]
+        return total, copies
+
+    total, copies = exchange(part_ref, got, low, groups, 0)
+    held[...] = total
+    total, more = exchange(held, got_far, high, groups_far, near)
+    out_ref[...] = total
+    for copy in copies + more:
+        copy.wait_send()
 
 
 def pair_total(part, pair_count):
     bits = pair_count.bit_length() - 1
+    near = 1 << ((bits + 1) // 2)
+    far = pair_count // near
     return pl.pallas_call(
-        functools.partial(total_kernel, bits),
+        functools.partial(total_kernel, near, far),
         out_shape=jax.ShapeDtypeStruct(part.shape, jnp.float32),
         in_specs=[pl.BlockSpec(memory_space=pltpu.VMEM)],
         out_specs=pl.BlockSpec(memory_space=pltpu.VMEM),
         scratch_shapes=[
-            pltpu.VMEM((bits + 1,) + part.shape, jnp.float32),
-            pltpu.VMEM((bits,) + part.shape, jnp.float32),
-            pltpu.SemaphoreType.DMA((bits,)),
-            pltpu.SemaphoreType.DMA((bits,)),
+            pltpu.VMEM(part.shape, jnp.float32),
+            pltpu.VMEM((near,) + part.shape, jnp.float32),
+            pltpu.VMEM((far,) + part.shape, jnp.float32),
+            pltpu.SemaphoreType.DMA((near + far,)),
+            pltpu.SemaphoreType.DMA((near + far,)),
         ],
         compiler_params=pltpu.CompilerParams(collective_id=1, has_side_effects=True),
     )(part)
@@ -236,7 +286,7 @@
     weight = pair_weights(energy_bins, bin_weights, pair_local * pair_count)
     column_slab = lax.dynamic_slice_in_dim(
         pair_density_matrices, sigma_pos * col_count, col_count, 1
-    )
+    ) if self_energy_count > 1 else None
     polar_block = -polar_rows(pair_density_matrices, column_slab, weight, pair_count)
     coulomb_root = jnp.sqrt(coulomb)
     root_rows = lax.dynamic_slice_in_dim(coulomb_root, pair_position * row_count, row_count, 0)

time: 140 us -> 120 us (0.86)
  local copies, waits for them, and re-layouts: 18.5 us -> 3.27 us
  Pallas kernels: 112 us -> 107 us
    unnamed x9 -> x4, local copies, waits for them, and re-layouts: 11.5 us -> 2.82 us
    transpose x1 -> x0, local copies, waits for them, and re-layouts: 6.6 us -> none  [polar_rows(): pair_rows.reshape(pairs, pair_count // 2, 2, rows).transpose(2, 1, 3, 0)]
    pallas_call x2, Pallas kernels: 112 us -> 107 us  [the longest x1 95.2 us: polar_rows(): pl.pallas_call(functools.partial(polar_kernel, bits, orders, lags, None i...]
where the time goes in v2:
time: 120 us
  Pallas kernels  107 us (89%)
  matrix products  5.55 us (5%)
  other arithmetic  3.64 us (3%)
  local copies, waits for them, and re-layouts  3.27 us (3%)
    pallas_call x1, Pallas kernels, polar_rows(): pl.pallas_call(functools.partial(polar_kernel, bits, orders, lags, None i...  95.2 us
    pallas_call x1, Pallas kernels, pair_total(): pl.pallas_call(functools.partial(total_kernel, near, far), out_shape=jax....  11.4 us
    dot_general x1, matrix products, local(): jnp.einsum('frc,cn->rfn', lax.all_gather(screened, 'sigma', axis=2, tiled...  5.55 us
    unnamed x4, local copies, waits for them, and re-layouts  2.82 us

profile of v2, /device:TPU:0, one launch (start us, length us, event | category | flops | bytes accessed | tf_op | source)
XLA Modules:
  0.0 119.8 jit_solution(9848198467207744747)
XLA Ops:
  0.6 1.0 dynamic-slice_convert_fusion
  1.6 1.0 select_reduce_fusion
  2.6 0.4 copy.11
  3.0 1.1 broadcast_multiply_fusion.refs_0_
  4.0 0.0 copy-start
  4.0 95.2 %shard_map.68 = f32[2,48,1536]{2,1,0:T(8,128)} custom-call(bf16[2048,1536]{1,0:T(8,128)(2,1)} %full_ref.1, f32[2048,2]{1,0:T(8,128)} %broadcast_multiply_fusion.refs_0_), custom_call_target="tpu_custom_call" | custom-call | flops 19327352832 | bytes 12582912 | tf_op jit(solution)/shard_map/pallas_call | solution.py:174
  99.3 0.0 copy-done
  99.3 0.1 dynamic_slice.7
  99.4 5.6 %multiply_reduce_fusion = (f32[2,2048]{1,0:T(2,128)S(1)}, f32[48,2,2048]{2,0,1:T(8,128)S(1)}) fusion(f32[48,2048]{1,0:T(8,128)S(1)} %dynamic-slice_convert_fusion, bf16[1536,2048]{1,0:T(8,128)(2,1)} %param.9, f32[2,48,1536]{2,1,0:T(8,128)} %shard_map.68, f32[1536]{0:T(1024)S(1)} %sqrt.3, f32[48]{0:T(128)S(1)} %dynamic_slice.7), kind=kOutput, calls=%fused_computation.5 | convolution fusion | flops 3624710144 | bytes 8083648 | tf_op jit(solution)/shard_map/frc,cn->rfn/dot_general | solution.py:298
  105.0 1.5 %copy.13 = f32[48,2,2048]{2,1,0:T(2,128)} copy(f32[48,2,2048]{2,0,1:T(8,128)S(1)} %get-tuple-element.9) | data formatting | bytes 1572864
  106.4 0.6 broadcast_multiply_fusion.1.part_ref
  107.1 11.4 %shard_map.69 = f32[2,2048]{1,0:T(2,128)} custom-call(f32[2,2048]{1,0:T(2,128)} %broadcast_multiply_fusion.1.part_ref), custom_call_target="tpu_custom_call" | custom-call | tf_op jit(solution)/shard_map/pallas_call | solution.py:262
  118.5 1.3 %copy.15 = f32[2,2048]{1,0:T(2,128)} copy(f32[2,2048]{1,0:T(2,128)} %shard_map.69) | data formatting | bytes 32768
  (1 shorter events, 0.0 us)
Async XLA Ops:
  4.0 95.2 %copy-start = (f32[1536]{0:T(1024)S(1)}, f32[1536]{0:T(1024)}, u32[]{:S(2)}) copy-start(f32[1536]{0:T(1024)} %param.8) | copy-start | bytes 18436
